TPU v7x, 256 devices: a whole 4x4x8 slice. The times are simulated.
256 devices in a mesh: ep: 8 (over y, core), seq: 32 (over z, x).
Axes of the slice: x: 4, y: 4, z: 8, core: 2. Of those that a mesh axis runs over, the one named last changes fastest.
Arguments:
- frames: bfloat16 [8, 22528, 512], P('ep', 'seq'), may hold values from -6 to 6
- lengths: int32 [8], P('ep'), may hold values from 11264 to 22528
- w_in: bfloat16 [512, 1024], replicated, may hold values from -0.25 to 0.25
- kernel: float32 [31, 512], replicated, may hold values from -1 to 1
- w_out: bfloat16 [512, 512], replicated, may hold values from -0.25 to 0.25
- pool_query: bfloat16 [8, 512], replicated, may hold values from -600 to 600
- w_value: bfloat16 [512, 512], replicated, may hold values from -0.25 to 0.25
- text_emb: bfloat16 [256, 512], replicated, may hold values from -6 to 6
- teacher: float32 [8, 256], P('ep'), may hold values from -6 to 6
Outputs:
- loss: float32 [], replicated
- grad_in: float32 [512, 1024], P('seq', 'ep')
- grad_out: float32 [512, 512], P('seq', 'ep')
- grad_kernel: float32 [31, 512], replicated
- grad_query: float32 [8, 512], replicated
- grad_value: float32 [512, 512], replicated
All inputs are finite; a program needn't handle non-finite values.
Results may differ from a plain program's by a relative error of at most 0.03.
Values may be sent and summed in bfloat16 or wider, within the bound.
No kernel may reach another device: no remote copies, remote signals or barrier semaphores. Data moves between devices by JAX's collectives and lax.ppermute only.
A program may use at most 64 MiB of HBM per device.

v0:
```python
import jax
import jax.numpy as jnp
from jax import lax
from jax.sharding import PartitionSpec as P


def padded_2(block, sides, width):
    for axis, dim in sides:
        count = lax.axis_size(axis)
        forward = [(i, i + 1) for i in range(count - 1)]
        backward = [(target, source) for source, target in forward]
        low = lax.ppermute(
            lax.slice_in_dim(block, block.shape[dim] - width, None, axis=dim), axis, forward
        )
        high = lax.ppermute(lax.slice_in_dim(block, 0, width, axis=dim), axis, backward)
        block = jnp.concatenate([low, block, high], axis=dim)
    return block


def shards(frames, lengths, w_in, kernel, w_out, pool_query, w_value, text_emb, teacher):
    hi = lax.Precision.HIGHEST
    n_epis, n_rows, width = frames.shape
    n_taps = kernel.shape[0]
    rim = n_taps // 2
    n_heads = pool_query.shape[0]
    head_dim = width // n_heads
    n_cands = text_emb.shape[0]
    root_width = jnp.sqrt(jnp.float32(width))
    offset = lax.axis_index("seq") * n_rows
    positions = offset + jnp.arange(n_rows, dtype=jnp.int32)
    valid = (positions[None, :] < lengths[:, None]).astype(jnp.float32)[..., None]
    xf = frames.astype(jnp.float32)
    mean_val = jnp.mean(xf, axis=-1, keepdims=True)
    var_val = jnp.mean((xf - mean_val) ** 2, axis=-1, keepdims=True)
    normed = ((xf - mean_val) * lax.rsqrt(var_val + 1e-05)).astype(jnp.bfloat16)
    mixed = jnp.einsum("esd,df->esf", normed, w_in, preferred_element_type=jnp.float32)
    sig = jax.nn.sigmoid(mixed[..., width:])
    glu = (mixed[..., :width] * sig * valid).astype(jnp.bfloat16)
    padded = padded_2(glu, (("seq", 1),), rim)
    conv = jnp.zeros((n_epis, n_rows, width), jnp.float32)
    for k in range(n_taps):
        conv = conv + kernel[k] * padded[:, k : k + n_rows].astype(jnp.float32)
    sconv = jax.nn.sigmoid(conv)
    act = (conv * sconv).astype(jnp.bfloat16)
    resid = xf + jnp.einsum("esd,df->esf", act, w_out, preferred_element_type=jnp.float32)
    queries = pool_query.astype(jnp.float32)
    scores = jnp.einsum("esd,hd->esh", resid, queries, precision=hi) / root_width
    masked = jnp.where(valid > 0, scores, -1e30)
    top = lax.pmax(jnp.max(masked, axis=1), "seq")
    expo = jnp.where(valid > 0, jnp.exp(masked - top[:, None]), 0.0)
    vec_here = jnp.einsum("esh,esd->ehd", expo, resid, precision=hi)
    total, vec = lax.psum((jnp.sum(expo, axis=1), vec_here), "seq")
    probs = jnp.where(valid > 0, jnp.exp(masked - top[:, None]), 0.0) / total[:, None]
    vbar = vec / total[..., None]
    wvals = w_value.astype(jnp.float32).reshape(width, n_heads, head_dim)
    pooled = jnp.einsum("ehd,dhk->ehk", vbar, wvals, precision=hi).reshape(n_epis, width)
    rms = jnp.sqrt(jnp.mean(pooled * pooled, axis=-1, keepdims=True) + 1e-06)
    emb = pooled / rms
    texts = text_emb.astype(jnp.float32)
    score = jnp.einsum("ed,cd->ec", emb, texts, precision=hi) / root_width
    diff = score - teacher
    loss_here = jnp.sum(diff * diff) / n_cands
    dscore = 2.0 * diff / n_cands
    demb = jnp.einsum("ec,cd->ed", dscore, texts, precision=hi) / root_width
    dpooled = (demb - emb * jnp.mean(demb * emb, axis=-1, keepdims=True)) / rms
    dp3 = dpooled.reshape(n_epis, n_heads, head_dim)
    value_here = jnp.einsum("ehd,ehk->dhk", vbar, dp3, precision=hi).reshape(width, width)
    dvbar = jnp.einsum("dhk,ehk->ehd", wvals, dp3, precision=hi)
    proj = jnp.einsum("esd,ehd->esh", resid, dvbar, precision=hi)
    centre = jnp.sum(dvbar * vbar, axis=-1)
    dscores = probs * (proj - centre[:, None])
    query_here = jnp.einsum("esh,esd->hd", dscores, resid, precision=hi) / root_width
    dresid = (
        jnp.einsum("esh,ehd->esd", probs, dvbar, precision=hi)
        + jnp.einsum("esh,hd->esd", dscores, queries, precision=hi) / root_width
    ).astype(jnp.bfloat16)
    out_here = jnp.einsum("esd,esf->df", act, dresid, preferred_element_type=jnp.float32)
    dact = jnp.einsum("esf,df->esd", dresid, w_out, preferred_element_type=jnp.float32)
    dconv = (dact * sconv * (1.0 + conv * (1.0 - sconv))).astype(jnp.bfloat16)
    dconv_f = dconv.astype(jnp.float32)
    dpad = padded_2(dconv, (("seq", 1),), rim)
    dglu = jnp.zeros((n_epis, n_rows, width), jnp.float32)
    taps = []
    for k in range(n_taps):
        dglu = dglu + kernel[k] * dpad[:, 2 * rim - k : 2 * rim - k + n_rows].astype(jnp.float32)
        taps.append(jnp.sum(padded[:, k : k + n_rows].astype(jnp.float32) * dconv_f, axis=(0, 1)))
    kernel_here = jnp.stack(taps)
    dglu = dglu * valid
    dmixed = jnp.concatenate(
        [dglu * sig, dglu * mixed[..., :width] * sig * (1.0 - sig)], axis=-1
    ).astype(jnp.bfloat16)
    in_here = jnp.einsum("esd,esf->df", normed, dmixed, preferred_element_type=jnp.float32)
    rows_in, rows_out = (
        lax.psum_scatter(
            in_here.astype(jnp.bfloat16), "seq", scatter_dimension=0, tiled=True
        ).astype(jnp.float32),
        lax.psum_scatter(
            out_here.astype(jnp.bfloat16), "seq", scatter_dimension=0, tiled=True
        ).astype(jnp.float32),
    )
    grad_in, grad_out = (
        lax.psum_scatter(
            rows_in.astype(jnp.bfloat16), "ep", scatter_dimension=1, tiled=True
        ).astype(jnp.float32),
        lax.psum_scatter(
            rows_out.astype(jnp.bfloat16), "ep", scatter_dimension=1, tiled=True
        ).astype(jnp.float32),
    )
    grad_kernel, grad_query = lax.psum((kernel_here, query_here), ("ep", "seq"))
    grad_value, loss = (
        lax.psum(value_here.astype(jnp.bfloat16), "ep").astype(jnp.float32),
        lax.psum(loss_here.astype(jnp.bfloat16), "ep").astype(jnp.float32),
    )
    return (loss, grad_in, grad_out, grad_kernel, grad_query, grad_value)


def solution(mesh):
    return jax.shard_map(
        shards,
        mesh=mesh,
        in_specs=(P("ep", "seq", None), P("ep"), P(), P(), P(), P(), P(), P(), P("ep", None)),
        out_specs=(P(), P("seq", "ep"), P("seq", "ep"), P(), P(), P()),
        check_vma=False,
    )
```

profile of v0, /device:TPU:1, one launch (start us, length us, event | category | flops | bytes accessed | tf_op | source)
XLA Modules:
  0.0 1106.2 jit_solution(10548095060268716896)
XLA Ops:
  8.0 1.3 convert_reduce_fusion
  9.3 1.5 fusion.5
  10.8 0.6 copy-done.88
  11.4 1.0 convolution_bitcast_fusion
  12.8 1.1 copy-done.3
  14.0 3.9 collective-permute-start
  17.9 1.3 collective-permute-start.1
  19.6 1.0 copy.20
  20.6 1.8 collective-permute-done.1
  22.6 9.4 fusion.36
  32.1 0.6 fusion.37
  33.2 0.9 fusion.189
  34.1 62.9 %pmax.7 = f32[8]{0:T(128)S(1)} all-reduce(f32[8]{0:T(128)S(1)} %get-tuple-element.101), channel_id=1, replica_groups=mesh['ep'=8,'seq'=32] {'seq'}, use_global_device_ids=true, to_apply=%region_3.4 | all-reduce | flops 8 | bytes 64 | tf_op jit(solution)/shard_map/pmax | solution.py:49
  97.0 0.7 fusion.164
  97.7 0.8 convolution_bitcast_fusion.3
  98.5 111.0 %all-reduce.1 = (f32[1,8,512]{2,1,0:T(8,128)}, f32[8]{0:T(128)S(1)}) all-reduce(f32[1,8,512]{2,1,0:T(8,128)S(1)} %convolution_bitcast_fusion.3, f32[8]{0:T(128)} %fusion.164), channel_id=1, replica_groups=mesh['ep'=8,'seq'=32] {'seq'}, use_global_device_ids=true, to_apply=%region_4.5 | all-reduce | flops 4104 | bytes 32832 | tf_op jit(solution)/shard_map/psum | solution.py:52
  209.5 0.9 fusion.180
  210.4 1.5 fusion.161
  211.9 0.6 multiply_reduce_fusion
  213.3 0.7 broadcast_divide_fusion.1
  213.9 0.7 div.113
  214.6 0.7 reshape.298
  215.3 1.0 fusion.190
  216.3 0.9 fusion.171
  217.2 1.3 multiply_reduce_fusion.1
  219.1 0.7 subtract_divide_fusion
  219.9 1.4 fusion.191
  221.3 0.9 fusion.181
  222.1 2.1 fusion.159
  224.3 2.0 fusion.94
  226.3 0.8 fusion.93
  227.1 0.5 copy-done.9
  227.7 2.1 fusion.67
  229.9 0.9 copy-done.1
  230.8 1.3 collective-permute-start.2
  232.4 4.2 collective-permute-start.3
  236.5 1.4 convolution_convert_fusion.1
  238.4 25.7 %fusion.96 = (bf16[704,512]{1,0:T(8,128)(2,1)S(1)}, f32[1,704,512]{2,1,0:T(8,128)S(1)}) fusion(f32[1,704,1024]{2,1,0:T(8,128)} %copy-done.3, f32[704]{0:T(1024)S(1)} %copy-done.15, bf16[1,704,512]{2,1,0:T(8,128)(2,1)} %copy-done.1, bf16[1,15,512]{2,1,0:T(8,128)(2,1)S(1)} %collective-permute-done.3, f32[512]{0:T(512)S(1)} %bitcast.173, f32[512]{0:T(512)S(1)} %bitcast.175, ...), kind=kLoop, calls=%fused_computation.235 | loop fusion | flops 67764224 | bytes 4422400 | tf_op jit(solution)/shard_map/concatenate | solution.py:89
  264.1 0.6 fusion.97
  265.2 2.1 convolution_convert_fusion
  267.5 1.0 multiply_convert_fusion.4
  268.5 2.5 fusion.82
  271.1 1.7 fusion.84
  272.8 1.5 fusion.83
  274.3 216.4 %reduce-scatter.11.cloned.1.call-done = bf16[16,512]{1,0:T(8,128)(2,1)} async-done(((bf16[512,512]{1,0:T(8,128)(2,1)}), bf16[16,512]{1,0:T(8,128)(2,1)}) %reduce-scatter.11.cloned.1.call-update) | async-done | bytes 16400 | tf_op jit(solution)/shard_map/reduce_scatter | solution.py:97
  490.6 1.5 copy.28
  492.2 2.2 fusion.68
  494.4 213.8 %reduce-scatter.9.cloned.1.call-done = bf16[16,1024]{1,0:T(8,128)(2,1)} async-done(((bf16[512,1024]{1,0:T(8,128)(2,1)}), bf16[16,1024]{1,0:T(8,128)(2,1)}) %reduce-scatter.9.cloned.1.call-update) | async-done | bytes 32784 | tf_op jit(solution)/shard_map/reduce_scatter | solution.py:94
  708.2 1.6 copy.26
  709.9 1.4 convolution_multiply_fusion.2
  711.3 2.5 stack.127
  713.9 0.6 multiply_reduce_fusion.2
  715.1 18.4 %psum.44 = bf16[]{:T(256)} all-reduce(bf16[]{:T(256)S(6)} %div.117), channel_id=1, replica_groups=mesh['ep'=8,'seq'=32] {'ep'}, use_global_device_ids=true, to_apply=%region_9.10 | all-reduce | flops 1 | bytes 4 | tf_op jit(solution)/shard_map/psum | solution.py:112
  734.2 44.1 %all-reduce.5.cloned.1.call-done = bf16[512,512]{0,1:T(8,128)(2,1)} async-done(((bf16[512,512]{0,1:T(8,128)(2,1)}), bf16[512,512]{0,1:T(8,128)(2,1)}) %all-reduce.5.cloned.1.call-update) | async-done | bytes 524304 | tf_op jit(solution)/shard_map/psum | solution.py:111
  778.2 2.2 copy.21
  780.4 32.0 %reduce-scatter.15.cloned.1.call-done = bf16[64,16]{1,0:T(8,128)(2,1)} async-done(((bf16[512,16]{1,0:T(8,128)(2,1)}), bf16[64,16]{1,0:T(8,128)(2,1)}) %reduce-scatter.15.cloned.1.call-update) | async-done | bytes 2064
  812.4 0.8 copy.29
  813.2 0.6 convert_element_type.365
  813.8 33.0 %reduce-scatter.13.cloned.1.call-done = bf16[128,16]{1,0:T(8,128)(2,1)} async-done(((bf16[1024,16]{1,0:T(8,128)(2,1)}), bf16[128,16]{1,0:T(8,128)(2,1)}) %reduce-scatter.13.cloned.1.call-update) | async-done | bytes 4112
  846.8 0.8 copy.27
  847.6 0.6 convert_element_type.363
  848.3 247.1 %all-reduce.7.cloned.1.call-done = (f32[31,512]{1,0:T(8,128)}, f32[8,512]{1,0:T(8,128)}) async-done(((f32[31,512]{1,0:T(8,128)}, f32[8,512]{1,0:T(8,128)}), (f32[31,512]{1,0:T(8,128)}, f32[8,512]{1,0:T(8,128)})) %all-reduce.7.cloned.1.call-update) | async-done | bytes 79888 | tf_op jit(solution)/shard_map/psum | solution.py:109
  1095.4 1.5 copy.45
  1096.9 1.3 copy.46
  (207 shorter events, 2.5 us)
Async XLA Ops:
  7.2 4.2 copy-start
  7.2 4.2 copy-start.5
  7.2 483.4 %reduce-scatter.11.cloned.1.call-start = ((), (), s32[]{:S(2)}) async-start(), calls=%async_computation.5 | async-start | bytes 540672 | tf_op jit(solution)/shard_map/reduce_scatter | solution.py:97
  12.4 6.8 copy-start.13
  12.4 7.2 copy-start.11
  14.0 6.7 collective-permute-start
  17.9 4.5 collective-permute-start.1
  19.2 3.1 copy-start.18
  19.3 3.1 copy-start.20
  19.3 3.1 copy-start.28
  19.3 3.1 copy-start.30
  19.3 3.1 copy-start.32
  19.3 3.1 copy-start.34
  19.3 3.1 copy-start.36
  19.3 12.7 %copy-start.22 = (f32[1,512]{1,0:T(1,128)}, f32[1,512]{1,0:T(1,128)S(1)}, u32[]{:S(2)}) copy-start(f32[1,512]{1,0:T(1,128)S(1)} %get-tuple-element.89) | copy-start | bytes 6148
  19.3 12.7 %copy-start.24 = (f32[1,512]{1,0:T(1,128)}, f32[1,512]{1,0:T(1,128)S(1)}, u32[]{:S(2)}) copy-start(f32[1,512]{1,0:T(1,128)S(1)} %get-tuple-element.90) | copy-start | bytes 6148
  19.4 12.7 %copy-start.26 = (f32[1,512]{1,0:T(1,128)}, f32[1,512]{1,0:T(1,128)S(1)}, u32[]{:S(2)}) copy-start(f32[1,512]{1,0:T(1,128)S(1)} %get-tuple-element.91) | copy-start | bytes 6148
  20.6 11.5 %copy-start.6 = (bf16[1,704,512]{2,1,0:T(8,128)(2,1)S(1)}, bf16[1,704,512]{2,1,0:T(8,128)(2,1)}, u32[]{:S(2)}) copy-start(bf16[1,704,512]{2,1,0:T(8,128)(2,1)} %param.9) | copy-start | bytes 2162692
  20.6 11.5 %copy-start.90 = (bf16[512,512]{1,0:T(8,128)(2,1)S(1)}, bf16[512,512]{1,0:T(8,128)(2,1)}, u32[]{:S(2)}) copy-start(bf16[512,512]{1,0:T(8,128)(2,1)} %param.13) | copy-start | bytes 1572868
  34.1 181.2 %copy-start.10 = (bf16[256,512]{1,0:T(8,128)(2,1)S(1)}, bf16[256,512]{1,0:T(8,128)(2,1)}, u32[]{:S(2)}) copy-start(bf16[256,512]{1,0:T(8,128)(2,1)} %param.16) | copy-start | bytes 786436
  209.5 11.7 %copy-start.12 = (f32[1,8,512]{2,1,0:T(8,128)S(1)}, f32[1,8,512]{2,1,0:T(8,128)}, u32[]{:S(2)}) copy-start(f32[1,8,512]{2,1,0:T(8,128)} %get-tuple-element.60) | copy-start | bytes 49156
  222.1 4.1 copy-start.17
  230.8 7.3 collective-permute-start.2
  232.0 6.0 copy-start.15
  232.1 6.0 copy-start.19
  232.1 6.0 copy-start.21
  232.1 6.0 copy-start.23
  232.1 6.0 copy-start.25
  232.1 6.0 copy-start.27
  232.1 6.0 copy-start.29
  232.1 6.0 copy-start.31
  232.1 6.0 copy-start.33
  232.1 6.0 copy-start.35
  232.1 6.0 copy-start.37
  232.2 6.0 copy-start.39
  232.2 6.0 copy-start.41
  232.2 6.0 copy-start.43
  232.2 6.0 copy-start.45
  232.2 6.0 copy-start.47
  232.2 6.0 copy-start.49
  232.2 6.0 copy-start.51
  232.2 6.0 copy-start.53
  232.2 6.0 copy-start.55
  232.2 6.0 copy-start.57
  232.3 6.0 copy-start.59
  232.3 6.0 copy-start.61
  232.3 6.0 copy-start.63
  232.3 6.0 copy-start.65
  232.3 6.0 copy-start.67
  232.3 6.0 copy-start.69
  232.3 6.0 copy-start.71
  232.3 6.0 copy-start.73
  232.3 6.0 copy-start.75
  232.3 6.0 copy-start.77
  232.4 6.0 copy-start.79
  232.4 5.7 collective-permute-start.3
  238.0 470.2 %reduce-scatter.9.cloned.1.call-start = ((), (), s32[]{:S(2)}) async-start(), calls=%async_computation.4 | async-start | bytes 1081344 | tf_op jit(solution)/shard_map/reduce_scatter | solution.py:94
  238.1 26.0 %copy-start.4 = (f32[1,704,1024]{2,1,0:T(8,128)S(1)}, f32[1,704,1024]{2,1,0:T(8,128)}, u32[]{:S(2)}) copy-start(f32[1,704,1024]{2,1,0:T(8,128)} %copy-done.3) | copy-start | bytes 8650756
  267.4 510.9 %all-reduce.5.cloned.1.call-start = ((), (), s32[]{:S(2)}) async-start(), calls=%async_computation.6 | async-start | bytes 1048576 | tf_op jit(solution)/shard_map/psum | solution.py:111
  268.5 544.0 %reduce-scatter.15.cloned.1.call-start = ((), (), s32[]{:S(2)}) async-start(), calls=%async_computation.8 | async-start | bytes 147456
  492.1 354.7 %reduce-scatter.13.cloned.1.call-start = ((), (), s32[]{:S(2)}) async-start(), calls=%async_computation.7 | async-start | bytes 294912
  494.4 219.4 %copy-start.84 = (f32[256]{0:T(256)S(1)}, f32[256]{0:T(256)}, u32[]{:S(2)}) copy-start(f32[256]{0:T(256)} %copy-done.83) | copy-start | bytes 3076
  494.4 219.4 %copy-start.87 = (f32[1,256]{1,0:T(1,128)S(1)}, f32[1,256]{1,0:T(1,128)}, u32[]{:S(2)}) copy-start(f32[1,256]{1,0:T(1,128)} %param.17) | copy-start | bytes 3076
  709.8 385.6 %all-reduce.7.cloned.1.call-start = ((), (), s32[]{:S(2)}) async-start(), calls=%async_computation.9 | async-start | bytes 163840 | tf_op jit(solution)/shard_map/psum | solution.py:109
  (38 other events, 84.5 us)
Sparse Core Ops, SparseCore 0:
  238.1 252.4 reduce-scatter.10
  495.5 212.6 reduce-scatter.8
  710.6 67.5 all-reduce.4
  780.6 31.8 reduce-scatter.14
  814.9 31.8 reduce-scatter.12
  852.8 242.5 all-reduce.6
where the time goes:
time: 1110 us
  waiting for transfers between devices  788 us (71%)
  blocking collectives  192 us (17%)
  other arithmetic  55.3 us (5%)
  between operations  20.1 us (2%)
  matrix products  20 us (2%)
  local copies, waits for them, and re-layouts  19.4 us (2%)
    psum x1, waiting for transfers between devices, shards(): grad_kernel, grad_query = lax.psum((kernel_here, query_here), ('ep', 'seq'))  247 us
    reduce_scatter x1, waiting for transfers between devices, shards(): lax.psum_scatter(out_here.astype(jnp.bfloat16), 'seq', scatter_dimension=...  216 us
    reduce_scatter x1, waiting for transfers between devices, shards(): lax.psum_scatter(in_here.astype(jnp.bfloat16), 'seq', scatter_dimension=0...  214 us
    psum x1, blocking collectives, shards(): total, vec = lax.psum((jnp.sum(expo, axis=1), vec_here), 'seq')  111 us
    unnamed x8, waiting for transfers between devices  65.1 us
    pmax x1, blocking collectives, shards(): top = lax.pmax(jnp.max(masked, axis=1), 'seq')  62.9 us
    psum x1, waiting for transfers between devices, shards(): lax.psum(value_here.astype(jnp.bfloat16), 'ep').astype(jnp.float32)  44.1 us
    concatenate x2, other arithmetic, shards(): jnp.concatenate([dglu * sig, dglu * mixed[..., :width] * sig * (1.0 - sig...  26.3 us
  transfers between devices with their start and end apart: 10, of which 7 were waited for; matrix products, arithmetic and copies ran while one was open for 5% of the time, Pallas kernels for 0%

commit v1 on v0

--- a/solution.py
+++ b/solution.py
@@ -2,6 +2,9 @@
 import jax.numpy as jnp
 from jax import lax
 from jax.sharding import PartitionSpec as P
+from jax.lax import all_gather
+
+views_step_on = lambda piece_in, device_axis: all_gather(piece_in, device_axis).sum(axis=0)
 
 
 def padded_2(block, sides, width):
@@ -108,7 +111,7 @@
     )
     grad_kernel, grad_query = lax.psum((kernel_here, query_here), ("ep", "seq"))
     grad_value, loss = (
-        lax.psum(value_here.astype(jnp.bfloat16), "ep").astype(jnp.float32),
+        views_step_on(value_here.astype(jnp.bfloat16), "ep").astype(jnp.float32),
         lax.psum(loss_here.astype(jnp.bfloat16), "ep").astype(jnp.float32),
     )
     return (loss, grad_in, grad_out, grad_kernel, grad_query, grad_value)

time: 1110 us -> 981 us (0.88)
  waiting for transfers between devices: 788 us -> 659 us
    psum x1, waiting for transfers between devices: 247 us -> 146 us  [shards(): grad_kernel, grad_query = lax.psum((kernel_here, query_here), ('ep', 'seq'))]
    psum x1 -> x0, waiting for transfers between devices: 44.1 us -> none  [shards(): lax.psum(value_here.astype(jnp.bfloat16), 'ep').astype(jnp.float32)]
    all_gather x0 -> x1, waiting for transfers between devices: none -> 36.9 us  [all_gather(piece_in, device_axis).sum(axis=0)]
    unnamed x8, waiting for transfers between devices: 65.1 us -> 34.8 us
  transfers between devices with their start and end apart: 10 -> 10, of which waited for: 7 -> 7; matrix products, arithmetic and copies ran while one was open for 5% -> 6% of each run, Pallas kernels for 0% -> 0%
where the time goes in v1:
time: 981 us; the launch traced here: 980 us
  waiting for transfers between devices  659 us (67%)
  blocking collectives  191 us (19%)
  other arithmetic  58.8 us (6%)
  between operations  21.3 us (2%)
  matrix products  19.9 us (2%)
  local copies, waits for them, and re-layouts  19.1 us (2%)
  starting transfers between devices  10.9 us (1%)
    reduce_scatter x1, waiting for transfers between devices, shards(): lax.psum_scatter(out_here.astype(jnp.bfloat16), 'seq', scatter_dimension=...  224 us
    reduce_scatter x1, waiting for transfers between devices, shards(): lax.psum_scatter(in_here.astype(jnp.bfloat16), 'seq', scatter_dimension=0...  216 us
    psum x1, waiting for transfers between devices, shards(): grad_kernel, grad_query = lax.psum((kernel_here, query_here), ('ep', 'seq'))  146 us
    psum x1, blocking collectives, shards(): total, vec = lax.psum((jnp.sum(expo, axis=1), vec_here), 'seq')  110 us
    pmax x1, blocking collectives, shards(): top = lax.pmax(jnp.max(masked, axis=1), 'seq')  62.9 us
    all_gather x1, waiting for transfers between devices, all_gather(piece_in, device_axis).sum(axis=0)  36.9 us
    unnamed x8, waiting for transfers between devices  34.8 us
    concatenate x2, other arithmetic, shards(): jnp.concatenate([dglu * sig, dglu * mixed[..., :width] * sig * (1.0 - sig...  26.8 us
  transfers between devices with their start and end apart: 10, of which 7 were waited for; matrix products, arithmetic and copies ran while one was open for 6% of the time, Pallas kernels for 0%

profile of v1, /device:TPU:1, one launch (start us, length us, event | category | flops | bytes accessed | tf_op | source)
XLA Modules:
  0.0 980.2 jit_solution(1881273549521119915)
XLA Ops:
  8.8 1.3 convert_reduce_fusion
  10.2 1.5 fusion.5
  12.2 1.0 convolution_bitcast_fusion
  13.7 1.1 copy-done.3
  14.8 3.9 collective-permute-start
  18.7 1.3 collective-permute-start.1
  20.5 1.0 copy.20
  21.5 1.8 collective-permute-done.1
  23.2 9.3 fusion.36
  32.9 0.6 fusion.37
  34.0 0.9 fusion.189
  34.8 62.9 %pmax.7 = f32[8]{0:T(128)S(1)} all-reduce(f32[8]{0:T(128)S(1)} %get-tuple-element.83), channel_id=1, replica_groups=mesh['ep'=8,'seq'=32] {'seq'}, use_global_device_ids=true, to_apply=%region_3.4 | all-reduce | flops 8 | bytes 64 | tf_op jit(solution)/shard_map/pmax | solution.py:52
  97.7 0.7 fusion.164
  98.4 0.8 convolution_bitcast_fusion.3
  99.2 110.2 %all-reduce.1 = (f32[1,8,512]{2,1,0:T(8,128)}, f32[8]{0:T(128)S(1)}) all-reduce(f32[1,8,512]{2,1,0:T(8,128)S(1)} %convolution_bitcast_fusion.3, f32[8]{0:T(128)} %fusion.164), channel_id=1, replica_groups=mesh['ep'=8,'seq'=32] {'seq'}, use_global_device_ids=true, to_apply=%region_4.5 | all-reduce | flops 4104 | bytes 32832 | tf_op jit(solution)/shard_map/psum | solution.py:55
  209.5 0.9 fusion.180
  210.3 1.5 fusion.161
  211.9 0.6 multiply_reduce_fusion
  213.2 0.7 broadcast_divide_fusion.1
  213.9 0.6 div.113
  214.5 0.7 reshape.308
  215.2 1.0 fusion.190
  216.2 0.9 fusion.171
  217.1 1.3 multiply_reduce_fusion.1
  219.0 0.6 subtract_divide_fusion
  219.7 1.4 fusion.191
  221.1 0.8 fusion.181
  221.9 2.1 fusion.159
  224.0 1.9 fusion.94
  226.0 0.8 fusion.93
  227.4 2.2 fusion.67
  229.6 0.9 copy-done.1
  230.4 1.3 collective-permute-start.2
  232.0 4.2 collective-permute-start.3
  236.2 1.5 convolution_convert_fusion.1
  238.1 26.2 %fusion.96 = (bf16[704,512]{1,0:T(8,128)(2,1)S(1)}, f32[1,704,512]{2,1,0:T(8,128)S(1)}) fusion(f32[1,704,1024]{2,1,0:T(8,128)} %copy-done.3, f32[704]{0:T(1024)S(1)} %copy-done.15, bf16[1,704,512]{2,1,0:T(8,128)(2,1)} %copy-done.1, bf16[1,15,512]{2,1,0:T(8,128)(2,1)S(1)} %collective-permute-done.3, f32[512]{0:T(512)S(1)} %bitcast.173, f32[512]{0:T(512)S(1)} %bitcast.175, ...), kind=kLoop, calls=%fused_computation.235 | loop fusion | flops 67764224 | bytes 4422400 | tf_op jit(solution)/shard_map/concatenate | solution.py:92
  264.3 0.6 fusion.97
  265.4 2.1 convolution_convert_fusion
  267.6 223.6 %reduce-scatter.11.cloned.1.call-done = bf16[16,512]{1,0:T(8,128)(2,1)} async-done(((bf16[512,512]{1,0:T(8,128)(2,1)}), bf16[16,512]{1,0:T(8,128)(2,1)}) %reduce-scatter.11.cloned.1.call-update) | async-done | bytes 16400 | tf_op jit(solution)/shard_map/reduce_scatter | solution.py:100
  491.2 1.5 copy.28
  492.8 215.7 %reduce-scatter.9.cloned.1.call-done = bf16[16,1024]{1,0:T(8,128)(2,1)} async-done(((bf16[512,1024]{1,0:T(8,128)(2,1)}), bf16[16,1024]{1,0:T(8,128)(2,1)}) %reduce-scatter.9.cloned.1.call-update) | async-done | bytes 32784 | tf_op jit(solution)/shard_map/reduce_scatter | solution.py:97
  708.5 1.6 copy.26
  710.2 0.9 multiply_convert_fusion.4
  711.1 2.0 copy.21
  713.3 2.3 fusion.68
  715.6 1.5 fusion.82
  717.1 1.5 fusion.83
  718.6 1.7 fusion.84
  720.3 2.5 stack.127
  722.8 1.4 convolution_multiply_fusion.2
  724.3 0.6 multiply_reduce_fusion.2
  725.5 18.3 %psum.37 = bf16[]{:T(256)} all-reduce(bf16[]{:T(256)S(6)} %div.117), channel_id=1, replica_groups=mesh['ep'=8,'seq'=32] {'ep'}, use_global_device_ids=true, to_apply=%region_9.10 | all-reduce | flops 1 | bytes 4 | tf_op jit(solution)/shard_map/psum | solution.py:115
  744.5 1.0 reduce-scatter.15.cloned.1.call-done
  745.5 0.8 copy.29
  746.3 0.6 convert_element_type.374
  746.9 33.7 %reduce-scatter.13.cloned.1.call-done = bf16[128,16]{1,0:T(8,128)(2,1)} async-done(((bf16[1024,16]{1,0:T(8,128)(2,1)}), bf16[128,16]{1,0:T(8,128)(2,1)}) %reduce-scatter.13.cloned.1.call-update) | async-done | bytes 4112
  780.6 0.8 copy.27
  781.4 0.6 convert_element_type.372
  782.0 36.9 %all-gather.2.cloned.1.call-done = bf16[8,512,512]{2,1,0:T(8,128)(2,1)} async-done(((bf16[1,512,512]{2,1,0:T(8,128)(2,1)}), bf16[8,512,512]{2,1,0:T(8,128)(2,1)}) %all-gather.2.cloned.1.call-update) | async-done | bytes 4194320 | tf_op jit(solution)/shard_map/all_gather | solution.py:7
  819.0 3.1 reduce_sum.395
  822.0 1.1 convert_element_type.378
  823.2 146.0 %all-reduce.4.cloned.1.call-done = (f32[31,512]{1,0:T(8,128)}, f32[8,512]{1,0:T(8,128)}) async-done(((f32[31,512]{1,0:T(8,128)}, f32[8,512]{1,0:T(8,128)}), (f32[31,512]{1,0:T(8,128)}, f32[8,512]{1,0:T(8,128)})) %all-reduce.4.cloned.1.call-update) | async-done | bytes 79888 | tf_op jit(solution)/shard_map/psum | solution.py:112
  969.1 1.5 copy.44
  970.6 1.3 copy.45
  (209 shorter events, 3.6 us)
Async XLA Ops:
  8.0 483.2 %reduce-scatter.11.cloned.1.call-start = ((), (), s32[]{:S(2)}) async-start(), calls=%async_computation.5 | async-start | bytes 540672 | tf_op jit(solution)/shard_map/reduce_scatter | solution.py:100
  13.2 6.8 copy-start.13
  13.2 7.2 copy-start.11
  14.8 6.7 collective-permute-start
  18.7 4.5 collective-permute-start.1
  20.1 12.5 %copy-start.22 = (f32[1,512]{1,0:T(1,128)}, f32[1,512]{1,0:T(1,128)S(1)}, u32[]{:S(2)}) copy-start(f32[1,512]{1,0:T(1,128)S(1)} %get-tuple-element.71) | copy-start | bytes 6148
  20.1 12.5 %copy-start.24 = (f32[1,512]{1,0:T(1,128)}, f32[1,512]{1,0:T(1,128)S(1)}, u32[]{:S(2)}) copy-start(f32[1,512]{1,0:T(1,128)S(1)} %get-tuple-element.72) | copy-start | bytes 6148
  20.1 12.5 %copy-start.26 = (f32[1,512]{1,0:T(1,128)}, f32[1,512]{1,0:T(1,128)S(1)}, u32[]{:S(2)}) copy-start(f32[1,512]{1,0:T(1,128)S(1)} %get-tuple-element.73) | copy-start | bytes 6148
  20.1 12.5 %copy-start.28 = (f32[1,512]{1,0:T(1,128)}, f32[1,512]{1,0:T(1,128)S(1)}, u32[]{:S(2)}) copy-start(f32[1,512]{1,0:T(1,128)S(1)} %get-tuple-element.74) | copy-start | bytes 6148
  20.1 12.5 %copy-start.30 = (f32[1,512]{1,0:T(1,128)}, f32[1,512]{1,0:T(1,128)S(1)}, u32[]{:S(2)}) copy-start(f32[1,512]{1,0:T(1,128)S(1)} %get-tuple-element.75) | copy-start | bytes 6148
  20.1 12.5 %copy-start.32 = (f32[1,512]{1,0:T(1,128)}, f32[1,512]{1,0:T(1,128)S(1)}, u32[]{:S(2)}) copy-start(f32[1,512]{1,0:T(1,128)S(1)} %get-tuple-element.76) | copy-start | bytes 6148
  20.2 12.5 %copy-start.34 = (f32[1,512]{1,0:T(1,128)}, f32[1,512]{1,0:T(1,128)S(1)}, u32[]{:S(2)}) copy-start(f32[1,512]{1,0:T(1,128)S(1)} %get-tuple-element.77) | copy-start | bytes 6148
  20.2 12.5 %copy-start.36 = (f32[1,512]{1,0:T(1,128)}, f32[1,512]{1,0:T(1,128)S(1)}, u32[]{:S(2)}) copy-start(f32[1,512]{1,0:T(1,128)S(1)} %get-tuple-element.78) | copy-start | bytes 6148
  20.2 12.5 %copy-start.38 = (f32[1,512]{1,0:T(1,128)}, f32[1,512]{1,0:T(1,128)S(1)}, u32[]{:S(2)}) copy-start(f32[1,512]{1,0:T(1,128)S(1)} %get-tuple-element.79) | copy-start | bytes 6148
  20.2 12.5 %copy-start.40 = (f32[1,512]{1,0:T(1,128)}, f32[1,512]{1,0:T(1,128)S(1)}, u32[]{:S(2)}) copy-start(f32[1,512]{1,0:T(1,128)S(1)} %get-tuple-element.80) | copy-start | bytes 6148
  20.2 12.4 %copy-start.42 = (f32[1,512]{1,0:T(1,128)}, f32[1,512]{1,0:T(1,128)S(1)}, u32[]{:S(2)}) copy-start(f32[1,512]{1,0:T(1,128)S(1)} %get-tuple-element.50) | copy-start | bytes 6148
  20.2 12.4 %copy-start.44 = (f32[1,512]{1,0:T(1,128)}, f32[1,512]{1,0:T(1,128)S(1)}, u32[]{:S(2)}) copy-start(f32[1,512]{1,0:T(1,128)S(1)} %get-tuple-element.51) | copy-start | bytes 6148
  20.3 12.4 %copy-start.46 = (f32[1,512]{1,0:T(1,128)}, f32[1,512]{1,0:T(1,128)S(1)}, u32[]{:S(2)}) copy-start(f32[1,512]{1,0:T(1,128)S(1)} %get-tuple-element.52) | copy-start | bytes 6148
  20.3 12.4 %copy-start.48 = (f32[1,512]{1,0:T(1,128)}, f32[1,512]{1,0:T(1,128)S(1)}, u32[]{:S(2)}) copy-start(f32[1,512]{1,0:T(1,128)S(1)} %get-tuple-element.53) | copy-start | bytes 6148
  20.3 12.4 %copy-start.50 = (f32[1,512]{1,0:T(1,128)}, f32[1,512]{1,0:T(1,128)S(1)}, u32[]{:S(2)}) copy-start(f32[1,512]{1,0:T(1,128)S(1)} %get-tuple-element.54) | copy-start | bytes 6148
  20.3 12.4 %copy-start.52 = (f32[1,512]{1,0:T(1,128)}, f32[1,512]{1,0:T(1,128)S(1)}, u32[]{:S(2)}) copy-start(f32[1,512]{1,0:T(1,128)S(1)} %get-tuple-element.55) | copy-start | bytes 6148
  20.3 12.4 %copy-start.54 = (f32[1,512]{1,0:T(1,128)}, f32[1,512]{1,0:T(1,128)S(1)}, u32[]{:S(2)}) copy-start(f32[1,512]{1,0:T(1,128)S(1)} %get-tuple-element.56) | copy-start | bytes 6148
  20.3 12.4 %copy-start.56 = (f32[1,512]{1,0:T(1,128)}, f32[1,512]{1,0:T(1,128)S(1)}, u32[]{:S(2)}) copy-start(f32[1,512]{1,0:T(1,128)S(1)} %get-tuple-element.57) | copy-start | bytes 6148
  20.3 12.4 %copy-start.58 = (f32[1,512]{1,0:T(1,128)}, f32[1,512]{1,0:T(1,128)S(1)}, u32[]{:S(2)}) copy-start(f32[1,512]{1,0:T(1,128)S(1)} %get-tuple-element.58) | copy-start | bytes 6148
  20.3 12.4 %copy-start.60 = (f32[1,512]{1,0:T(1,128)}, f32[1,512]{1,0:T(1,128)S(1)}, u32[]{:S(2)}) copy-start(f32[1,512]{1,0:T(1,128)S(1)} %get-tuple-element.59) | copy-start | bytes 6148
  20.3 12.4 %copy-start.62 = (f32[1,512]{1,0:T(1,128)}, f32[1,512]{1,0:T(1,128)S(1)}, u32[]{:S(2)}) copy-start(f32[1,512]{1,0:T(1,128)S(1)} %get-tuple-element.60) | copy-start | bytes 6148
  20.3 12.4 %copy-start.64 = (f32[1,512]{1,0:T(1,128)}, f32[1,512]{1,0:T(1,128)S(1)}, u32[]{:S(2)}) copy-start(f32[1,512]{1,0:T(1,128)S(1)} %get-tuple-element.61) | copy-start | bytes 6148
  20.4 12.4 %copy-start.66 = (f32[1,512]{1,0:T(1,128)}, f32[1,512]{1,0:T(1,128)S(1)}, u32[]{:S(2)}) copy-start(f32[1,512]{1,0:T(1,128)S(1)} %get-tuple-element.62) | copy-start | bytes 6148
  20.4 12.4 %copy-start.68 = (f32[1,512]{1,0:T(1,128)}, f32[1,512]{1,0:T(1,128)S(1)}, u32[]{:S(2)}) copy-start(f32[1,512]{1,0:T(1,128)S(1)} %get-tuple-element.63) | copy-start | bytes 6148
  20.4 12.4 %copy-start.70 = (f32[1,512]{1,0:T(1,128)}, f32[1,512]{1,0:T(1,128)S(1)}, u32[]{:S(2)}) copy-start(f32[1,512]{1,0:T(1,128)S(1)} %get-tuple-element.64) | copy-start | bytes 6148
  20.4 12.4 %copy-start.72 = (f32[1,512]{1,0:T(1,128)}, f32[1,512]{1,0:T(1,128)S(1)}, u32[]{:S(2)}) copy-start(f32[1,512]{1,0:T(1,128)S(1)} %get-tuple-element.65) | copy-start | bytes 6148
  20.4 12.4 %copy-start.74 = (f32[1,512]{1,0:T(1,128)}, f32[1,512]{1,0:T(1,128)S(1)}, u32[]{:S(2)}) copy-start(f32[1,512]{1,0:T(1,128)S(1)} %get-tuple-element.66) | copy-start | bytes 6148
  20.4 12.4 %copy-start.76 = (f32[1,512]{1,0:T(1,128)}, f32[1,512]{1,0:T(1,128)S(1)}, u32[]{:S(2)}) copy-start(f32[1,512]{1,0:T(1,128)S(1)} %get-tuple-element.67) | copy-start | bytes 6148
  20.4 12.4 %copy-start.78 = (f32[1,512]{1,0:T(1,128)}, f32[1,512]{1,0:T(1,128)S(1)}, u32[]{:S(2)}) copy-start(f32[1,512]{1,0:T(1,128)S(1)} %get-tuple-element.68) | copy-start | bytes 6148
  21.5 11.4 %copy-start.6 = (bf16[1,704,512]{2,1,0:T(8,128)(2,1)S(1)}, bf16[1,704,512]{2,1,0:T(8,128)(2,1)}, u32[]{:S(2)}) copy-start(bf16[1,704,512]{2,1,0:T(8,128)(2,1)} %param.9) | copy-start | bytes 2162692
  21.5 11.4 %copy-start.90 = (bf16[512,512]{1,0:T(8,128)(2,1)S(1)}, bf16[512,512]{1,0:T(8,128)(2,1)}, u32[]{:S(2)}) copy-start(bf16[512,512]{1,0:T(8,128)(2,1)} %param.13) | copy-start | bytes 1572868
  34.8 180.3 %copy-start.10 = (bf16[256,512]{1,0:T(8,128)(2,1)S(1)}, bf16[256,512]{1,0:T(8,128)(2,1)}, u32[]{:S(2)}) copy-start(bf16[256,512]{1,0:T(8,128)(2,1)} %param.16) | copy-start | bytes 786436
  209.5 11.6 %copy-start.12 = (f32[1,8,512]{2,1,0:T(8,128)S(1)}, f32[1,8,512]{2,1,0:T(8,128)}, u32[]{:S(2)}) copy-start(f32[1,8,512]{2,1,0:T(8,128)} %get-tuple-element.42) | copy-start | bytes 49156
  230.4 7.3 collective-permute-start.2
  231.7 6.1 copy-start.15
  231.7 6.1 copy-start.19
  231.7 6.1 copy-start.21
  231.8 6.1 copy-start.23
  231.8 6.1 copy-start.25
  231.8 6.1 copy-start.27
  231.8 6.1 copy-start.29
  231.8 6.1 copy-start.31
  231.8 6.1 copy-start.33
  231.8 6.1 copy-start.35
  231.8 6.1 copy-start.37
  231.8 6.1 copy-start.39
  231.8 6.1 copy-start.41
  231.9 6.1 copy-start.43
  231.9 6.1 copy-start.45
  231.9 6.1 copy-start.47
  231.9 6.1 copy-start.49
  231.9 6.1 copy-start.51
  232.0 5.7 collective-permute-start.3
  237.7 470.8 %reduce-scatter.9.cloned.1.call-start = ((), (), s32[]{:S(2)}) async-start(), calls=%async_computation.4 | async-start | bytes 1081344 | tf_op jit(solution)/shard_map/reduce_scatter | solution.py:97
  237.8 26.5 %copy-start.4 = (f32[1,704,1024]{2,1,0:T(8,128)S(1)}, f32[1,704,1024]{2,1,0:T(8,128)}, u32[]{:S(2)}) copy-start(f32[1,704,1024]{2,1,0:T(8,128)} %copy-done.3) | copy-start | bytes 8650756
  267.6 478.0 %reduce-scatter.15.cloned.1.call-start = ((), (), s32[]{:S(2)}) async-start(), calls=%async_computation.8 | async-start | bytes 147456
  492.7 287.9 %reduce-scatter.13.cloned.1.call-start = ((), (), s32[]{:S(2)}) async-start(), calls=%async_computation.7 | async-start | bytes 294912
  710.2 108.8 %all-gather.2.cloned.1.call-start = ((), (), s32[]{:S(2)}) async-start(), calls=%async_computation.6 | async-start | bytes 4718592 | tf_op jit(solution)/shard_map/all_gather | solution.py:7
  713.2 255.9 %all-reduce.4.cloned.1.call-start = ((), (), s32[]{:S(2)}) async-start(), calls=%async_computation.9 | async-start | bytes 163840 | tf_op jit(solution)/shard_map/psum | solution.py:112
  (38 other events, 135.0 us)
Sparse Core Ops, SparseCore 0:
  237.8 253.3 reduce-scatter.10
  496.1 212.4 reduce-scatter.8
  711.2 34.3 reduce-scatter.14
  747.9 32.6 reduce-scatter.12
  782.5 36.4 all-gather.1
Sparse Core Ops, SparseCore 1:
  724.3 244.7 all-reduce.3
